TPU v7x, 32 devices: a whole 2x2x4 slice. The times are simulated.
32 devices in a mesh: pairs: 2 (over x), tgt: 16 (over z, y, core).
Axes of the slice: x: 2, y: 2, z: 4, core: 2. Of those that a mesh axis runs over, the one named last changes fastest.
Arguments:
- src_hidden: bfloat16 [4096, 128], P(('pairs', 'tgt')), parts along dimension 0, may hold values from -6 to 6
- tgt_hidden: bfloat16 [256, 256, 128], P(('pairs', 'tgt')), parts along dimension 0, may hold values from -6 to 6
- proj_weight: bfloat16 [128, 256], replicated, may hold values from -0.5 to 0.5
- proj_bias: float32 [256], replicated, may hold values from -1.5 to 1.5
Outputs:
- level_one: bfloat16 [128, 128, 2048], P(('pairs', 'tgt')), parts along dimension 0
- level_two: bfloat16 [4096, 2048], P(('pairs', 'tgt')), parts along dimension 0
- level_three: bfloat16 [4096, 512], P(('pairs', 'tgt')), parts along dimension 0
There are 2 independent parts, one for each index of `pairs`. A program takes and returns all parts, laid end to end along the dimension named above; an argument that names none is the same for every part. Nothing has to cross between parts.
All inputs are finite; a program needn't handle non-finite values.
Results may differ from a plain program's by a relative error of at most 0.006.
Values may be sent and summed in bfloat16 or wider, within the bound.
A program may use at most 64 MiB of HBM per device.

v0:
```python
import math

import jax
import jax.numpy as jnp
from jax import lax
from jax.sharding import PartitionSpec as P


def project_features(hidden, weight, bias):
    result = jnp.dot(hidden, weight, preferred_element_type=jnp.float32) + bias
    return result.astype(jnp.bfloat16)


def pool_leading(values):
    height, across, depth = values.shape
    return values.reshape(height // 2, 2, across // 2, 2, depth).mean(axis=(1, 3))


def pool_trailing(values):
    depth, height, across = values.shape
    return values.reshape(depth, height // 2, 2, across // 2, 2).mean(axis=(2, 4))


def split_parts(values):
    upper = values.astype(jnp.bfloat16)
    lower = (values - upper.astype(jnp.float32)).astype(jnp.bfloat16)
    return (upper, lower)


def per_device(src_hidden, tgt_hidden, proj_weight, proj_bias):
    row_count, col_count, hidden_width = tgt_hidden.shape
    channels = proj_weight.shape[1]
    stripe_count = lax.axis_size("tgt")
    own_sources = src_hidden.shape[0]
    source_count = own_sources * stripe_count
    inverse_root = 1.0 / math.sqrt(channels)
    tgt_feat = project_features(
        tgt_hidden.reshape(row_count * col_count, hidden_width), proj_weight, proj_bias
    )
    grid_feat = tgt_feat.astype(jnp.float32).reshape(row_count, col_count, channels)
    fine_pool = pool_leading(grid_feat)
    coarse_pool = pool_leading(fine_pool)
    fine_upper, fine_lower = split_parts(fine_pool.reshape(-1, channels))
    coarse_upper, coarse_lower = split_parts(coarse_pool.reshape(-1, channels))
    own_features = project_features(src_hidden, proj_weight, proj_bias)
    all_features = lax.all_gather(own_features, "tgt", axis=0, tiled=True)
    block_size = 512
    block_total = source_count // block_size
    fine_count = fine_upper.shape[0]
    coarse_count = coarse_upper.shape[0]
    empty_levels = (
        jnp.zeros((fine_count, source_count), jnp.bfloat16),
        jnp.zeros((source_count, coarse_count), jnp.bfloat16),
    )
    contract_last = (((1,), (1,)), ((), ()))

    def one_block(block_index, levels):
        level_one, coarse_rows = levels
        offset = (block_index * block_size).astype(jnp.int32)
        panel = lax.dynamic_slice_in_dim(all_features, offset, block_size, 0)
        fine_corr = lax.dot_general(
            fine_upper, panel, contract_last, preferred_element_type=jnp.float32
        )
        fine_corr = fine_corr + lax.dot_general(
            fine_lower, panel, contract_last, preferred_element_type=jnp.float32
        )
        coarse_corr = lax.dot_general(
            panel, coarse_upper, contract_last, preferred_element_type=jnp.float32
        )
        coarse_corr = coarse_corr + lax.dot_general(
            panel, coarse_lower, contract_last, preferred_element_type=jnp.float32
        )
        zero_index = jnp.zeros((), jnp.int32)
        level_one = lax.dynamic_update_slice(
            level_one, (fine_corr * inverse_root).astype(jnp.bfloat16), (zero_index, offset)
        )
        coarse_rows = lax.dynamic_update_slice(
            coarse_rows, (coarse_corr * inverse_root).astype(jnp.bfloat16), (offset, zero_index)
        )
        return (level_one, coarse_rows)

    level_one, coarse_rows = lax.fori_loop(0, block_total, one_block, empty_levels)
    level_one = level_one.reshape(row_count // 2, col_count // 2, source_count)
    level_two = lax.all_to_all(coarse_rows, "tgt", split_axis=0, concat_axis=1, tiled=True)
    coarse_grid = level_two.astype(jnp.float32).reshape(
        own_sources, stripe_count * (row_count // 4), col_count // 4
    )
    level_three = pool_trailing(coarse_grid).reshape(own_sources, -1).astype(jnp.bfloat16)
    return (level_one, level_two, level_three)


def solution(mesh):
    return jax.shard_map(
        per_device,
        mesh=mesh,
        in_specs=(P(("pairs", "tgt"), None), P(("pairs", "tgt"), None, None), P(), P()),
        out_specs=(
            P(("pairs", "tgt"), None, None),
            P(("pairs", "tgt"), None),
            P(("pairs", "tgt"), None),
        ),
        check_vma=False,
    )
```

profile of v0, /device:TPU:0, one launch (start us, length us, event | category | flops | bytes accessed | tf_op | source)
XLA Modules:
  0.0 93.0 jit_solution(4818545377180773034)
XLA Ops:
  7.2 0.0 copy-start
  7.2 0.0 all-gather.2.cloned.1.call-start
  7.2 1.7 %fusion.18 = bf16[128,256]{1,0:T(8,128)(2,1)} fusion(bf16[128,128]{1,0:T(8,128)(2,1)} %param.6, bf16[128,256]{1,0:T(8,128)(2,1)} %param.8, f32[256]{0:T(256)} %param.9), kind=kOutput, calls=%fused_computation.23 | convolution fusion | flops 8454144 | bytes 164864 | tf_op jit(solution)/shard_map/dot_general | solution.py:10
  8.9 0.0 all-gather.2.cloned.1.call-update
  8.9 0.0 copy-done
  8.9 2.6 %fusion.17 = f32[2048,256]{1,0:T(8,128)} fusion(bf16[2048,128]{1,0:T(8,128)(2,1)S(1)} %bitcast.40, bf16[128,256]{1,0:T(8,128)(2,1)} %param.8, f32[256]{0:T(256)} %param.9), kind=kOutput, calls=%fused_computation.21 | convolution fusion | flops 135790592 | bytes 2688000 | tf_op jit(solution)/shard_map/dot_general | solution.py:10
  11.5 2.5 %reshape.38 = f32[4,2,128,2,256]{4,3,2,1,0:T(2,128)S(1)} reshape(f32[2048,256]{1,0:T(8,128)} %fusion.17) | data formatting | bytes 4194304 | tf_op jit(solution)/shard_map/reshape;reshape | solution.py:16
  14.0 1.5 %reduce_sum.27 = f32[4,128,256]{2,1,0:T(8,128)S(1)} reduce(f32[4,2,128,2,256]{4,3,2,1,0:T(2,128)S(1)} %reshape.38, f32[]{:T(128)} %constant.47.clone.1), dimensions={1,3}, to_apply=%region_0.0 | reduce | flops 393216 | bytes 2621444 | tf_op jit(solution)/shard_map/reduce_sum | solution.py:16
  15.5 0.3 div.27
  15.9 0.4 reduce_sum.28
  16.3 35.1 %all-gather.2.cloned.1.call-done = bf16[2048,256]{1,0:T(8,128)(2,1)} async-done(((bf16[128,256]{1,0:T(8,128)(2,1)}), bf16[2048,256]{1,0:T(8,128)(2,1)}) %all-gather.2.cloned.1.call-update) | async-done | bytes 1048592 | tf_op jit(solution)/shard_map/all_gather | solution.py:46
  51.4 0.0 copy-start.1
  51.4 0.9 broadcast_in_dim.9
  52.3 1.6 %broadcast_in_dim.8.clone = bf16[512,2048]{1,0:T(8,128)(2,1)} broadcast(bf16[]{:T(256)} %constant.46.clone.1), dimensions={} | broadcast | bytes 2097154 | tf_op jit(solution)/shard_map/broadcast_in_dim | solution.py:52
  53.9 0.0 copy-done.1
  53.9 11.4 %while.15 = (s32[]{:T(128)}, bf16[512,2048]{1,0:T(8,128)(2,1)}, bf16[2048,128]{1,0:T(8,128)(2,1)}, bf16[2048,256]{1,0:T(8,128)(2,1)S(1)}, bf16[512,256]{1,0:T(8,...) while((s32[]{:T(128)}, bf16[512,2048]{1,0:T(8,128)(2,1)}, ...), condition=%wide.region_3.0_spmd, body=%wide.region_2.0_spmd.sunk | while | flops 336527360 | bytes 7079091 | solution.py:82
  53.9 0.2 fusion.51
  54.1 0.9 fusion.52
  55.0 0.3 fusion.49
  55.3 0.3 fusion.50
  55.7 0.2 copy.30
  55.9 0.8 constant_dynamic-update-slice_fusion.2
  56.7 0.2 fusion.51
  56.9 0.9 fusion.52
  57.8 0.3 fusion.49
  58.2 0.3 fusion.50
  58.5 0.2 copy.30
  58.7 0.8 constant_dynamic-update-slice_fusion.2
  59.5 0.2 fusion.51
  59.8 0.9 fusion.52
  60.7 0.3 fusion.49
  61.0 0.3 fusion.50
  61.3 0.2 copy.30
  61.5 0.8 constant_dynamic-update-slice_fusion.2
  62.4 0.2 fusion.51
  62.6 0.9 fusion.52
  63.5 0.3 fusion.49
  63.8 0.3 fusion.50
  64.2 0.2 copy.30
  64.4 0.8 constant_dynamic-update-slice_fusion.2
  65.2 18.1 %all_to_all.19 = bf16[16,128,128]{2,1,0:T(8,128)(2,1)S(1)} all-to-all(bf16[16,128,128]{2,1,0:T(8,128)(2,1)} %bitcast.5), channel_id=1, replica_groups=mesh['pairs'=2,'tgt'=16] {'tgt'}, dimensions={0} | all-to-all | bytes 1048576 | tf_op jit(solution)/shard_map/all_to_all | solution.py:84
  83.3 0.3 copy.22
  83.6 1.0 %copy.25 = bf16[128,2048]{1,0:T(8,128)(2,1)} copy(bf16[128,2048]{0,1:T(8,128)(2,1)S(1)} %bitcast.44) | data formatting | bytes 1048576
  84.6 0.1 bitcast_convert_fusion.2
  84.7 0.5 copy.23
  85.2 0.1 reduce_sum.29
  85.4 0.8 copy.26
  (6 shorter events, 0.2 us)
Async XLA Ops:
  7.2 1.8 %copy-start = (bf16[8,256,128]{2,1,0:T(8,128)(2,1)S(1)}, bf16[8,256,128]{2,1,0:T(8,128)(2,1)}, u32[]{:S(2)}) copy-start(bf16[8,256,128]{2,1,0:T(8,128)(2,1)} %param.7) | copy-start | bytes 1572868
  7.2 44.2 %all-gather.2.cloned.1.call-start = ((), (), s32[]{:S(2)}) async-start(), calls=%async_computation.1 | async-start | bytes 1114112 | tf_op jit(solution)/shard_map/all_gather | solution.py:46
  51.4 2.4 %copy-start.1 = (bf16[2048,256]{1,0:T(8,128)(2,1)S(1)}, bf16[2048,256]{1,0:T(8,128)(2,1)}, u32[]{:S(2)}) copy-start(bf16[2048,256]{1,0:T(8,128)(2,1)} %all-gather.2.cloned.1.call-done) | copy-start | bytes 3145732
Sparse Core Ops, SparseCore 0:
  10.8 40.6 all-gather.1
where the time goes:
time: 93.3 us; the launch traced here: 93 us
  waiting for transfers between devices  35.1 us (38%)
  blocking collectives  18.1 us (19%)
  between operations  14.2 us (15%)
  local copies, waits for them, and re-layouts  12 us (13%)
  matrix products  11.3 us (12%)
  other arithmetic  2.17 us (2%)
    all_gather x1, waiting for transfers between devices, per_device(): all_features = lax.all_gather(own_features, 'tgt', axis=0, tiled=True)  35.1 us
    all_to_all x1, blocking collectives, per_device(): lax.all_to_all(coarse_rows, 'tgt', split_axis=0, concat_axis=1, tiled=True)  18.1 us
    dot_general x2, matrix products, project_features(): result = jnp.dot(hidden, weight, preferred_element_type=jnp.float32) + bias  4.25 us
    dynamic_update_slice x8, local copies, waits for them, and re-layouts, one_block(): lax.dynamic_update_slice(level_one, (fine_corr * inverse_root).astype(jnp...  4.19 us
    dot_general x4, matrix products, one_block(): lax.dot_general(panel, coarse_lower, contract_last, preferred_element_typ...  3.57 us
    another operation x1, local copies, waits for them, and re-layouts, pool_leading(): values.reshape(height // 2, 2, across // 2, 2, depth).mean(axis=(1, 3))  2.49 us
  transfers between devices with their start and end apart: 1, of which 1 were waited for; matrix products, arithmetic and copies ran while one was open for 8% of the time, Pallas kernels for 0%

commit v1 on v0

v1 whole, which is shorter than its diff:
```python
import functools
import math

import jax
import jax.numpy as jnp
from jax import lax
from jax.experimental import pallas as pl
from jax.experimental.pallas import tpu as pltpu
from jax.sharding import PartitionSpec as P

MESH = pl.DeviceIdType.MESH
LAST = (((1,), (1,)), ((), ()))


def dot(left, right):
    return jnp.dot(left, right, preferred_element_type=jnp.float32)


def dot_last(left, right):
    return lax.dot_general(left, right, LAST, preferred_element_type=jnp.float32)


def split_parts(values):
    upper = values.astype(jnp.bfloat16)
    lower = (values - upper.astype(jnp.float32)).astype(jnp.bfloat16)
    return upper, lower


def pool_matrix(window, width):
    shape = (width // window, window * width)
    out = lax.broadcasted_iota(jnp.int32, shape, 0)
    pixel = lax.broadcasted_iota(jnp.int32, shape, 1)
    inside = lax.div(lax.rem(pixel, width), window) == out
    return jnp.where(inside, 1.0 / (window * window), 0.0).astype(jnp.bfloat16)


def gather_kernel(count, scale, src_ref, tgt_ref, weight_ref, bias_ref,
                  all_ref, fine_ref, send_sem, recv_sem):
    rows, width, hidden = tgt_ref.shape
    lines = count // 4
    me = lax.axis_index("tgt")
    core = lax.rem(me, 2)
    mate = me + 1 - 2 * core
    side = lax.rem(lax.div(me, 2), 2)
    beside = me + 2 - 4 * side
    line = lax.div(me, 4)
    place = me - 4 * line

    def along(step):
        return 4 * lax.rem(line + step, lines) + place

    barrier = pltpu.get_barrier_semaphore()
    peers = [along(step) for step in range(1, lines)] + [beside, mate]
    for peer in peers:
        pl.semaphore_signal(barrier, inc=1, device_id={"tgt": peer}, device_id_type=MESH)
    all_ref[me, 0] = src_ref[...]
    pl.semaphore_wait(barrier, len(peers))

    sent = []

    def copy(part, block, peer, slot):
        return pltpu.make_async_remote_copy(
            src_ref=all_ref.at[block, part],
            dst_ref=all_ref.at[block, part],
            send_sem=send_sem.at[part, slot],
            recv_sem=recv_sem.at[part, block],
            device_id={"tgt": peer},
            device_id_type=MESH,
        )

    slots = [0, 0]

    def send(part, block, peer):
        one = copy(part, block, peer, slots[part])
        slots[part] += 1
        one.start()
        sent.append(one)

    def arrive(part, block):
        copy(part, block, mate, 0).wait_recv()

    def own(part):
        for step in range(1, lines):
            send(part, me, along(step))
        send(part, me, beside)
        send(part, me, mate)

    own(0)
    coarse = pool_matrix(4, width)
    pooled = []
    for row in range(0, rows, 4):
        pooled.append(dot(coarse, tgt_ref[row:row + 4].reshape(4 * width, hidden)))
    all_ref[me, 1] = jnp.concatenate(pooled, axis=0).astype(jnp.bfloat16)
    own(1)
    fine = pool_matrix(2, width)
    half = width // 2
    for row in range(0, rows, 2):
        upper, lower = split_parts(dot(fine, tgt_ref[row:row + 2].reshape(2 * width, hidden)))
        feat = dot(upper, weight_ref[...]) + dot(lower, weight_ref[...]) + bias_ref[...]
        fine_ref[row // 2 * half:(row // 2 + 1) * half] = (feat * scale).astype(jnp.bfloat16)
    for part in (0, 1):
        for step in range(1, lines):
            block = along(lines - step)
            arrive(part, block)
            send(part, block, beside)
            send(part, block, mate)
    for part in (0, 1):
        for step in range(lines):
            block = along((lines - step) % lines) + 2 - 4 * side
            arrive(part, block)
            send(part, block, mate)
    for part in (0, 1):
        for step in range(lines):
            block = along((lines - step) % lines) + 1 - 2 * core
            arrive(part, block)
            arrive(part, block + 2 - 4 * side)
    for one in sent:
        one.wait_send()


def level_kernel(scale, all_ref, fine_ref, src_ref, weight_ref, bias_ref,
                 one_ref, two_ref, three_ref, upper_ref, lower_ref, bias_dot_ref):
    group, _, block, hidden = all_ref.shape

    @pl.when(pl.program_id(0) == 0)
    def _():
        feat = (dot(src_ref[...], weight_ref[...]) + bias_ref[...]).astype(jnp.bfloat16)
        back = dot_last(feat, weight_ref[...]) * scale
        upper, lower = split_parts(back)
        upper_ref[...] = upper
        lower_ref[...] = lower
        shift = jnp.sum(feat.astype(jnp.float32) * bias_ref[...], axis=1, keepdims=True) * scale
        bias_dot_ref[...] = jnp.broadcast_to(shift, bias_dot_ref.shape)

    coarse = all_ref[:, 1].reshape(group * block, hidden)
    two = dot_last(upper_ref[...], coarse) + dot_last(lower_ref[...], coarse)
    two = (two + bias_dot_ref[:, :1]).astype(jnp.bfloat16)
    two_ref[...] = two
    wide = two_ref.shape[1]
    narrow = three_ref.shape[1]
    across = block // 2
    pixel = lax.broadcasted_iota(jnp.int32, (wide, narrow), 0)
    out = lax.broadcasted_iota(jnp.int32, (wide, narrow), 1)
    inside = (lax.div(pixel, block) * (across // 2) + lax.div(lax.rem(pixel, across), 2)) == out
    pool = jnp.where(inside, 0.25, 0.0).astype(jnp.bfloat16)
    three_ref[...] = dot(two, pool).astype(jnp.bfloat16)
    src = all_ref[:, 0].reshape(group * block, hidden)
    feat = (dot(src, weight_ref[...]) + bias_ref[...]).astype(jnp.bfloat16)
    one_ref[...] = dot_last(fine_ref[...], feat).astype(jnp.bfloat16)


def per_device(src_hidden, tgt_hidden, proj_weight, proj_bias):
    rows, width, hidden = tgt_hidden.shape
    channels = proj_weight.shape[1]
    count = lax.axis_size("tgt")
    own = src_hidden.shape[0]
    scale = 1.0 / math.sqrt(channels)
    fine_count = rows * width // 4
    bias = proj_bias.reshape(1, channels)
    vmem = pl.BlockSpec(memory_space=pltpu.VMEM)
    gathered, fine = pl.pallas_call(
        functools.partial(gather_kernel, count, scale),
        out_shape=(
            jax.ShapeDtypeStruct((count, 2, own, hidden), jnp.bfloat16),
            jax.ShapeDtypeStruct((fine_count, channels), jnp.bfloat16),
        ),
        in_specs=[vmem] * 4,
        out_specs=(vmem, vmem),
        scratch_shapes=[
            pltpu.SemaphoreType.DMA((2, count)),
            pltpu.SemaphoreType.DMA((2, count)),
        ],
        compiler_params=pltpu.CompilerParams(
            collective_id=0, has_side_effects=True, vmem_limit_bytes=32 * 1024 * 1024
        ),
        name="gather",
    )(src_hidden, tgt_hidden, proj_weight, bias)
    group = 4
    whole = lambda step: (0, 0)
    one, two, three = pl.pallas_call(
        functools.partial(level_kernel, scale),
        grid=(count // group,),
        out_shape=(
            jax.ShapeDtypeStruct((fine_count, own * count), jnp.bfloat16),
            jax.ShapeDtypeStruct((own, fine_count // 4 * count), jnp.bfloat16),
            jax.ShapeDtypeStruct((own, fine_count // 16 * count), jnp.bfloat16),
        ),
        in_specs=[
            pl.BlockSpec((group, 2, own, hidden), lambda step: (step, 0, 0, 0)),
            pl.BlockSpec((fine_count, channels), whole),
            pl.BlockSpec((own, hidden), whole),
            pl.BlockSpec((hidden, channels), whole),
            pl.BlockSpec((1, channels), whole),
        ],
        out_specs=(
            pl.BlockSpec((fine_count, own * group), lambda step: (0, step)),
            pl.BlockSpec((own, fine_count // 4 * group), lambda step: (0, step)),
            pl.BlockSpec((own, fine_count // 16 * group), lambda step: (0, step)),
        ),
        scratch_shapes=[
            pltpu.VMEM((own, hidden), jnp.bfloat16),
            pltpu.VMEM((own, hidden), jnp.bfloat16),
            pltpu.VMEM((own, 128), jnp.float32),
        ],
        compiler_params=pltpu.CompilerParams(vmem_limit_bytes=32 * 1024 * 1024),
        name="levels",
    )(gathered, fine, src_hidden, proj_weight, bias)
    return one.reshape(rows // 2, width // 2, own * count), two, three


def solution(mesh):
    return jax.shard_map(
        per_device,
        mesh=mesh,
        in_specs=(P(("pairs", "tgt"), None), P(("pairs", "tgt"), None, None), P(), P()),
        out_specs=(
            P(("pairs", "tgt"), None, None),
            P(("pairs", "tgt"), None),
            P(("pairs", "tgt"), None),
        ),
        check_vma=False,
    )
```

time: 93.3 us -> 24.8 us (0.27)
  waiting for transfers between devices: 35.1 us -> 0 us
  Pallas kernels: 0 us -> 20.5 us
  blocking collectives: 18.1 us -> 0 us
  between operations: 14.2 us -> 0.65 us
  matrix products: 11.3 us -> 0 us
  local copies, waits for them, and re-layouts: 12 us -> 3.31 us
  other arithmetic: 2.17 us -> 0 us
    all_gather x1 -> x0, waiting for transfers between devices: 35.1 us -> none  [per_device(): all_features = lax.all_gather(own_features, 'tgt', axis=0, tiled=True)]
    pallas_call x0 -> x2, Pallas kernels: none -> 20.5 us  [the longest x1 16.5 us: per_device(): pl.pallas_call(functools.partial(gather_kernel, count, scale), out_shape=...]
    all_to_all x1 -> x0, blocking collectives: 18.1 us -> none  [per_device(): lax.all_to_all(coarse_rows, 'tgt', split_axis=0, concat_axis=1, tiled=True)]
    dot_general x18 -> x0, matrix products: 11.3 us -> none  [the longest x2 4.25 us: project_features(): result = jnp.dot(hidden, weight, preferred_element_type=jnp.float32) + bias]
    dynamic_update_slice x8 -> x0, local copies, waits for them, and re-layouts: 4.19 us -> none  [one_block(): lax.dynamic_update_slice(level_one, (fine_corr * inverse_root).astype(jnp...]
    another operation x1 -> x0, local copies, waits for them, and re-layouts: 2.49 us -> none  [pool_leading(): values.reshape(height // 2, 2, across // 2, 2, depth).mean(axis=(1, 3))]
    broadcast_in_dim x2 -> x0, local copies, waits for them, and re-layouts: 2.43 us -> none  [the longest x1 1.57 us: per_device(): jnp.zeros((fine_count, source_count), jnp.bfloat16)]
    reduce_sum x3 -> x0, other arithmetic: 1.94 us -> none  [the longest x2 1.84 us: pool_leading(): values.reshape(height // 2, 2, across // 2, 2, depth).mean(axis=(1, 3))]
  transfers between devices with their start and end apart: 1 -> 0, of which waited for: 1 -> 0; matrix products, arithmetic and copies ran while one was open for 8% -> 0% of each run, Pallas kernels for 0% -> 0%
where the time goes in v1:
time: 24.8 us; the launch traced here: 24.5 us
  Pallas kernels  20.5 us (83%)
  local copies, waits for them, and re-layouts  3.31 us (13%)
  between operations  0.65 us (3%)
    pallas_call x1, Pallas kernels, per_device(): pl.pallas_call(functools.partial(gather_kernel, count, scale), out_shape=...  16.5 us
    pallas_call x1, Pallas kernels, per_device(): pl.pallas_call(functools.partial(level_kernel, scale), grid=(count // gro...  4.04 us
    unnamed x8, local copies, waits for them, and re-layouts  3.31 us

profile of v1, /device:TPU:0, one launch (start us, length us, event | category | flops | bytes accessed | tf_op | source)
XLA Modules:
  0.0 24.5 jit_solution(2131300218618015972)
XLA Ops:
  0.6 0.0 copy-start
  0.6 1.0 %copy-done = bf16[8,256,128]{2,1,0:T(8,128)(2,1)S(1)} copy-done((bf16[8,256,128]{2,1,0:T(8,128)(2,1)S(1)}, bf16[8,256,128]{2,1,0:T(8,128)(2,1)}, u32[]{:S(2)}) %copy-start) | copy-done | bytes 524312
  1.7 0.0 copy-start.1
  1.7 0.8 %copy-done.1 = bf16[128,256]{1,0:T(8,128)(2,1)S(1)} copy-done((bf16[128,256]{1,0:T(8,128)(2,1)S(1)}, bf16[128,256]{1,0:T(8,128)(2,1)}, u32[]{:S(2)}) %copy-start.1) | copy-done | bytes 65560
  2.5 0.0 copy-start.2
  2.5 0.8 %copy-done.2 = bf16[128,128]{1,0:T(8,128)(2,1)S(1)} copy-done((bf16[128,128]{1,0:T(8,128)(2,1)S(1)}, bf16[128,128]{1,0:T(8,128)(2,1)}, u32[]{:S(2)}) %copy-start.2) | copy-done | bytes 32792
  3.3 0.0 copy-start.3
  3.3 0.7 %copy-done.3 = f32[256]{0:T(256)S(1)} copy-done((f32[256]{0:T(256)S(1)}, f32[256]{0:T(256)}, u32[]{:S(2)}) %copy-start.3) | copy-done | bytes 1048
  4.0 16.5 %gather.1 = (bf16[16,2,128,128]{3,2,1,0:T(8,128)(2,1)S(1)}, bf16[512,256]{1,0:T(8,128)(2,1)S(1)}) custom-call(bf16[128,128]{1,0:T(8,128)(2,1)S(1)} %copy-done.2, bf16[8,256,128]{2,1,0:T(8,128)(2,1)S(1)} %copy-done, bf16[128,256]{1,0:T(8,128)(2,1)S(1)} %copy-done.1, f32[1,256]{1,0:T(1,128)S(1)} %bitcast.2), custom_call_target="tpu_custom_call" | custom-call | tf_op jit(solution)/shard_map/gather/pallas_call | solution.py:161
  20.4 4.0 %levels.1 = (bf16[512,2048]{1,0:T(8,128)(2,1)}, bf16[128,2048]{1,0:T(8,128)(2,1)}, bf16[128,512]{1,0:T(8,128)(2,1)}) custom-call(bf16[16,2,128,128]{3,2,1,0:T(8,128)(2,1)S(1)} %get-tuple-element.8.all_ref, bf16[512,256]{1,0:T(8,128)(2,1)S(1)} %get-tuple-element.9.fine_ref, bf16[128,128]{1,0:T(8,128)(2,1)S(1)} %copy-done.2, bf16[128,256]{1,0:T(8,128)(2,1)S(1)} %copy-done.1, ...), custom_call_target="tpu_custom_call" | custom-call | tf_op jit(solution)/shard_map/levels/pallas_call | solution.py:180
Async XLA Ops:
  0.6 1.0 %copy-start = (bf16[8,256,128]{2,1,0:T(8,128)(2,1)S(1)}, bf16[8,256,128]{2,1,0:T(8,128)(2,1)}, u32[]{:S(2)}) copy-start(bf16[8,256,128]{2,1,0:T(8,128)(2,1)} %tgt_ref.1) | copy-start | bytes 1572868
  1.7 0.8 %copy-start.1 = (bf16[128,256]{1,0:T(8,128)(2,1)S(1)}, bf16[128,256]{1,0:T(8,128)(2,1)}, u32[]{:S(2)}) copy-start(bf16[128,256]{1,0:T(8,128)(2,1)} %weight_ref.3) | copy-start | bytes 196612
  2.5 0.8 %copy-start.2 = (bf16[128,128]{1,0:T(8,128)(2,1)S(1)}, bf16[128,128]{1,0:T(8,128)(2,1)}, u32[]{:S(2)}) copy-start(bf16[128,128]{1,0:T(8,128)(2,1)} %src_ref.3) | copy-start | bytes 98308
  3.3 0.7 %copy-start.3 = (f32[256]{0:T(256)S(1)}, f32[256]{0:T(256)}, u32[]{:S(2)}) copy-start(f32[256]{0:T(256)} %param.7) | copy-start | bytes 3076

commit v2 on v1

v2 whole, which is shorter than its diff:
```python
import functools
import math

import jax
import jax.numpy as jnp
from jax import lax
from jax.experimental import pallas as pl
from jax.experimental.pallas import tpu as pltpu
from jax.sharding import PartitionSpec as P

MESH = pl.DeviceIdType.MESH
LAST = (((1,), (1,)), ((), ()))


def dot(left, right):
    return jnp.dot(left, right, preferred_element_type=jnp.float32)


def dot_last(left, right):
    return lax.dot_general(left, right, LAST, preferred_element_type=jnp.float32)


def split_parts(values):
    upper = values.astype(jnp.bfloat16)
    lower = (values - upper.astype(jnp.float32)).astype(jnp.bfloat16)
    return upper, lower


def pool_matrix(window, width):
    shape = (width // window, window * width)
    out = lax.broadcasted_iota(jnp.int32, shape, 0)
    pixel = lax.broadcasted_iota(jnp.int32, shape, 1)
    inside = lax.div(lax.rem(pixel, width), window) == out
    return jnp.where(inside, 1.0 / (window * window), 0.0).astype(jnp.bfloat16)


def gather_kernel(count, scale, src_hbm, tgt_hbm, weight_hbm, bias_hbm,
                  all_ref, one_ref, upper_ref, lower_ref, shift_ref,
                  tgt_ref, weight_ref, bias_ref, fine_ref, load_sem, send_sem, recv_sem):
    rows, width, hidden = tgt_ref.shape
    own = src_hbm.shape[0]
    lines = count // 4
    me = lax.axis_index("tgt")
    core = lax.rem(me, 2)
    to_mate = 1 - 2 * core
    side = lax.rem(lax.div(me, 2), 2)
    to_beside = 2 - 4 * side
    line = lax.div(me, 4)
    has_above = line + 1 < lines
    has_below = line > 0

    barrier = pltpu.get_barrier_semaphore()

    def greet(peer):
        pl.semaphore_signal(barrier, inc=1, device_id={"tgt": peer}, device_id_type=MESH)

    greet(me + to_mate)
    greet(me + to_beside)
    pl.when(has_above)(lambda: greet(me + 4))
    pl.when(has_below)(lambda: greet(me - 4))
    loads = [
        pltpu.make_async_copy(tgt_hbm, tgt_ref, load_sem.at[0]),
        pltpu.make_async_copy(weight_hbm, weight_ref, load_sem.at[1]),
        pltpu.make_async_copy(bias_hbm, bias_ref, load_sem.at[2]),
        pltpu.make_async_copy(src_hbm, all_ref.at[me, 0], load_sem.at[3]),
    ]
    for load in loads:
        load.start()
    links = 2 + jnp.where(has_above, 1, 0) + jnp.where(has_below, 1, 0)
    pl.semaphore_wait(barrier, links)

    sent = []
    slots = [0, 0]

    def copy(part, block, peer, slot, first=False):
        return pltpu.make_async_remote_copy(
            src_ref=src_hbm if first else all_ref.at[block, part],
            dst_ref=all_ref.at[block, part],
            send_sem=send_sem.at[part, slot],
            recv_sem=recv_sem.at[part, block],
            device_id={"tgt": peer},
            device_id_type=MESH,
        )

    def send(part, block, peer, when, first=False):
        slot = slots[part]
        slots[part] += 1
        go = lambda: copy(part, block, peer, slot, first).start()
        end = lambda: copy(part, block, peer, slot, first).wait_send()
        sent.append((when, end))
        return go

    def arrive(part, block):
        copy(part, block, me + to_mate, 0).wait_recv()

    def level_one(block):
        feat = (dot(all_ref[block, 0], weight_ref[...]) + bias_ref[...]).astype(jnp.bfloat16)
        at = pl.ds(pl.multiple_of(block * own, own), own)
        one_ref[:, at] = dot_last(fine_ref[...], feat).astype(jnp.bfloat16)
        return feat

    def own_block(part):
        first = part == 0
        pl.when(has_above)(send(part, me, me + 4, has_above, first))
        pl.when(has_below)(send(part, me, me - 4, has_below, first))
        send(part, me, me + to_beside, None, first)()
        send(part, me, me + to_mate, None, first)()

    own_block(0)
    coarse = pool_matrix(4, width)
    loads[0].wait()
    pooled = []
    for row in range(0, rows, 4):
        pooled.append(dot(coarse, tgt_ref[row:row + 4].reshape(4 * width, hidden)))
    all_ref[me, 1] = jnp.concatenate(pooled, axis=0).astype(jnp.bfloat16)
    own_block(1)
    fine = pool_matrix(2, width)
    half = width // 2
    for load in loads[1:]:
        load.wait()
    for row in range(0, rows, 2):
        upper, lower = split_parts(dot(fine, tgt_ref[row:row + 2].reshape(2 * width, hidden)))
        feat = dot(upper, weight_ref[...]) + dot(lower, weight_ref[...]) + bias_ref[...]
        fine_ref[row // 2 * half:(row // 2 + 1) * half] = (feat * scale).astype(jnp.bfloat16)
    feat = level_one(me)
    upper, lower = split_parts(dot_last(feat, weight_ref[...]) * scale)
    upper_ref[...] = upper
    lower_ref[...] = lower
    shift = jnp.sum(feat.astype(jnp.float32) * bias_ref[...], axis=1, keepdims=True) * scale
    shift_ref[...] = jnp.broadcast_to(shift, shift_ref.shape)

    def from_line(part, step, sign):
        block = me + 4 * step * sign
        there = (line >= step) if sign < 0 else (line + step < lines)
        onward = has_above if sign < 0 else has_below
        both = jnp.logical_and(there, onward)
        relay = send(part, block, me - 4 * sign, both)
        across = send(part, block, me + to_beside, there)
        inner = send(part, block, me + to_mate, there)

        @pl.when(there)
        def _():
            arrive(part, block)
            pl.when(onward)(relay)
            across()
            inner()

        if part == 0:
            return lambda: pl.when(there)(lambda: (level_one(block), None)[1])
        return lambda: None

    def from_beside(part, step, sign):
        block = me + to_beside + 4 * step * sign
        there = (line >= step) if sign < 0 else (line + step < lines)
        inner = send(part, block, me + to_mate, there)

        @pl.when(there)
        def _():
            arrive(part, block)
            inner()
            if part == 0:
                level_one(block)

    def beside_step(step):
        for part in (0, 1):
            from_beside(part, step, -1)
            if step:
                from_beside(part, step, 1)

    for step in range(1, lines):
        later = []
        for part in (0, 1):
            for sign in (-1, 1):
                later.append(from_line(part, step, sign))
        for work in later:
            work()
        beside_step(step - 1)
    beside_step(lines - 1)
    other = me + to_mate - 4 * line
    for part in (0, 1):
        for step in range(lines):
            for block in (other + 4 * step, other + 4 * step + to_beside):
                arrive(part, block)
                if part == 0:
                    level_one(block)
    for when, end in sent:
        if when is None:
            end()
        else:
            pl.when(when)(end)


def level_kernel(group, all_ref, one_ref, upper_ref, lower_ref, shift_ref,
                 one_hbm, two_hbm, three_hbm, two_ref, three_ref, sems):
    count, _, block, hidden = all_ref.shape
    rows = one_ref.shape[0] // 4
    copies = []

    def put(source, target):
        one = pltpu.make_async_copy(source, target, sems.at[len(copies)])
        one.start()
        copies.append(one)

    for part in range(4):
        at = pl.ds(part * rows, rows)
        put(one_ref.at[at], one_hbm.at[at])
    wide = group * block
    narrow = wide // 4
    across = block // 2
    pixel = lax.broadcasted_iota(jnp.int32, (wide, narrow), 0)
    out = lax.broadcasted_iota(jnp.int32, (wide, narrow), 1)
    inside = (lax.div(pixel, block) * (across // 2) + lax.div(lax.rem(pixel, across), 2)) == out
    pool = jnp.where(inside, 0.25, 0.0).astype(jnp.bfloat16)
    for step in range(count // group):
        coarse = all_ref[step * group:(step + 1) * group, 1].reshape(wide, hidden)
        two = dot_last(upper_ref[...], coarse) + dot_last(lower_ref[...], coarse)
        two = (two + shift_ref[:, :1]).astype(jnp.bfloat16)
        two_ref[:, step * wide:(step + 1) * wide] = two
        three_ref[:, step * narrow:(step + 1) * narrow] = dot(two, pool).astype(jnp.bfloat16)
    put(two_ref, two_hbm)
    put(three_ref, three_hbm)
    for one in copies:
        one.wait()


def per_device(src_hidden, tgt_hidden, proj_weight, proj_bias):
    rows, width, hidden = tgt_hidden.shape
    channels = proj_weight.shape[1]
    count = lax.axis_size("tgt")
    own = src_hidden.shape[0]
    scale = 1.0 / math.sqrt(channels)
    fine_count = rows * width // 4
    lines = count // 4
    bias = proj_bias.reshape(1, channels)
    vmem = pl.BlockSpec(memory_space=pltpu.VMEM)
    hbm = pl.BlockSpec(memory_space=pltpu.HBM)
    gathered, one, upper, lower, shift = pl.pallas_call(
        functools.partial(gather_kernel, count, scale),
        out_shape=(
            jax.ShapeDtypeStruct((count, 2, own, hidden), jnp.bfloat16),
            jax.ShapeDtypeStruct((fine_count, own * count), jnp.bfloat16),
            jax.ShapeDtypeStruct((own, hidden), jnp.bfloat16),
            jax.ShapeDtypeStruct((own, hidden), jnp.bfloat16),
            jax.ShapeDtypeStruct((own, 128), jnp.float32),
        ),
        in_specs=[hbm] * 4,
        out_specs=(vmem,) * 5,
        scratch_shapes=[
            pltpu.VMEM(tgt_hidden.shape, jnp.bfloat16),
            pltpu.VMEM(proj_weight.shape, jnp.bfloat16),
            pltpu.VMEM(bias.shape, jnp.float32),
            pltpu.VMEM((fine_count, channels), jnp.bfloat16),
            pltpu.SemaphoreType.DMA((4,)),
            pltpu.SemaphoreType.DMA((2, 4 + 6 * (lines - 1) + 2 * lines)),
            pltpu.SemaphoreType.DMA((2, count)),
        ],
        compiler_params=pltpu.CompilerParams(
            collective_id=0, has_side_effects=True, vmem_limit_bytes=32 * 1024 * 1024
        ),
        name="gather",
    )(src_hidden, tgt_hidden, proj_weight, bias)
    two_count = fine_count // 4 * count
    one, two, three = pl.pallas_call(
        functools.partial(level_kernel, 4),
        out_shape=(
            jax.ShapeDtypeStruct((fine_count, own * count), jnp.bfloat16),
            jax.ShapeDtypeStruct((own, two_count), jnp.bfloat16),
            jax.ShapeDtypeStruct((own, two_count // 4), jnp.bfloat16),
        ),
        in_specs=[vmem] * 5,
        out_specs=(hbm,) * 3,
        scratch_shapes=[
            pltpu.VMEM((own, two_count), jnp.bfloat16),
            pltpu.VMEM((own, two_count // 4), jnp.bfloat16),
            pltpu.SemaphoreType.DMA((6,)),
        ],
        compiler_params=pltpu.CompilerParams(vmem_limit_bytes=32 * 1024 * 1024),
        name="levels",
    )(gathered, one, upper, lower, shift)
    return one.reshape(rows // 2, width // 2, own * count), two, three


def solution(mesh):
    return jax.shard_map(
        per_device,
        mesh=mesh,
        in_specs=(P(("pairs", "tgt"), None), P(("pairs", "tgt"), None, None), P(), P()),
        out_specs=(
            P(("pairs", "tgt"), None, None),
            P(("pairs", "tgt"), None),
            P(("pairs", "tgt"), None),
        ),
        check_vma=False,
    )
```

time: 24.8 us -> 26.7 us (1.077)
  Pallas kernels: 20.5 us -> 22.5 us
    pallas_call x1, Pallas kernels: 16.5 us -> 20.7 us  [per_device(): pl.pallas_call(functools.partial(gather_kernel, count, scale), out_shape=...]
    pallas_call x1, Pallas kernels: 4.04 us -> 1.74 us  [per_device(): pl.pallas_call(functools.partial(level_kernel, 4), out_shape=(jax.ShapeDt...]
where the time goes in v2:
time: 26.7 us; the launch traced here: 26.4 us
  Pallas kernels  22.5 us (84%)
  local copies, waits for them, and re-layouts  3.31 us (12%)
  between operations  0.65 us (2%)
    pallas_call x1, Pallas kernels, per_device(): pl.pallas_call(functools.partial(gather_kernel, count, scale), out_shape=...  20.7 us
    unnamed x8, local copies, waits for them, and re-layouts  3.31 us
    pallas_call x1, Pallas kernels, per_device(): pl.pallas_call(functools.partial(level_kernel, 4), out_shape=(jax.ShapeDt...  1.74 us

profile of v2, /device:TPU:0, one launch (start us, length us, event | category | flops | bytes accessed | tf_op | source)
XLA Modules:
  0.0 26.4 jit_solution(13642197060152172253)
XLA Ops:
  0.6 0.0 copy-start
  0.6 1.0 %copy-done = bf16[8,256,128]{2,1,0:T(8,128)(2,1)S(1)} copy-done((bf16[8,256,128]{2,1,0:T(8,128)(2,1)S(1)}, bf16[8,256,128]{2,1,0:T(8,128)(2,1)}, u32[]{:S(2)}) %copy-start) | copy-done | bytes 524312
  1.7 0.0 copy-start.1
  1.7 0.8 %copy-done.1 = bf16[128,256]{1,0:T(8,128)(2,1)S(1)} copy-done((bf16[128,256]{1,0:T(8,128)(2,1)S(1)}, bf16[128,256]{1,0:T(8,128)(2,1)}, u32[]{:S(2)}) %copy-start.1) | copy-done | bytes 65560
  2.5 0.0 copy-start.2
  2.5 0.8 %copy-done.2 = bf16[128,128]{1,0:T(8,128)(2,1)S(1)} copy-done((bf16[128,128]{1,0:T(8,128)(2,1)S(1)}, bf16[128,128]{1,0:T(8,128)(2,1)}, u32[]{:S(2)}) %copy-start.2) | copy-done | bytes 32792
  3.3 0.0 copy-start.3
  3.3 0.7 %copy-done.3 = f32[256]{0:T(256)S(1)} copy-done((f32[256]{0:T(256)S(1)}, f32[256]{0:T(256)}, u32[]{:S(2)}) %copy-start.3) | copy-done | bytes 1048
  4.0 20.7 %gather.1 = (bf16[16,2,128,128]{3,2,1,0:T(8,128)(2,1)S(1)}, bf16[512,2048]{1,0:T(8,128)(2,1)S(1)}, bf16[128,128]{1,0:T(8,128)(2,1)S(1)}, bf16[128,128]{1,0:T(8,128)(2,1)S(1)}, f32[128,128]{1,0:T(8,128)S(1)}) custom-call(bf16[128,128]{1,0:T(8,128)(2,1)S(1)} %copy-done.2, bf16[8,256,128]{2,1,0:T(8,128)(2,1)S(1)} %copy-done, bf16[128,256]{1,0:T(8,128)(2,1)S(1)} %copy-done.1, ...), custom_call_target="tpu_custom_call" | custom-call | tf_op jit(solution)/shard_map/gather/pallas_call | solution.py:237
  24.7 1.7 %levels.1 = (bf16[512,2048]{1,0:T(8,128)(2,1)}, bf16[128,2048]{1,0:T(8,128)(2,1)}, bf16[128,512]{1,0:T(8,128)(2,1)}) custom-call(bf16[16,2,128,128]{3,2,1,0:T(8,128)(2,1)S(1)} %get-tuple-element.11.all_ref, bf16[512,2048]{1,0:T(8,128)(2,1)S(1)} %get-tuple-element.12.one_ref, bf16[128,128]{1,0:T(8,128)(2,1)S(1)} %get-tuple-element.13.upper_ref, ...), custom_call_target="tpu_custom_call" | custom-call | tf_op jit(solution)/shard_map/levels/pallas_call | solution.py:263
Async XLA Ops:
  0.6 1.0 %copy-start = (bf16[8,256,128]{2,1,0:T(8,128)(2,1)S(1)}, bf16[8,256,128]{2,1,0:T(8,128)(2,1)}, u32[]{:S(2)}) copy-start(bf16[8,256,128]{2,1,0:T(8,128)(2,1)} %tgt_hbm.1) | copy-start | bytes 1572868
  1.7 0.8 %copy-start.1 = (bf16[128,256]{1,0:T(8,128)(2,1)S(1)}, bf16[128,256]{1,0:T(8,128)(2,1)}, u32[]{:S(2)}) copy-start(bf16[128,256]{1,0:T(8,128)(2,1)} %weight_hbm.1) | copy-start | bytes 196612
  2.5 0.8 %copy-start.2 = (bf16[128,128]{1,0:T(8,128)(2,1)S(1)}, bf16[128,128]{1,0:T(8,128)(2,1)}, u32[]{:S(2)}) copy-start(bf16[128,128]{1,0:T(8,128)(2,1)} %src_hbm.1) | copy-start | bytes 98308
  3.3 0.7 %copy-start.3 = (f32[256]{0:T(256)S(1)}, f32[256]{0:T(256)}, u32[]{:S(2)}) copy-start(f32[256]{0:T(256)} %param.7) | copy-start | bytes 3076

commit v3 on v1

v3 whole, which is shorter than its diff:
```python
import functools
import math

import jax
import jax.numpy as jnp
from jax import lax
from jax.experimental import pallas as pl
from jax.experimental.pallas import tpu as pltpu
from jax.sharding import PartitionSpec as P

MESH = pl.DeviceIdType.MESH
LAST = (((1,), (1,)), ((), ()))


def dot(left, right):
    return jnp.dot(left, right, preferred_element_type=jnp.float32)


def dot_last(left, right):
    return lax.dot_general(left, right, LAST, preferred_element_type=jnp.float32)


def split_parts(values):
    upper = values.astype(jnp.bfloat16)
    lower = (values - upper.astype(jnp.float32)).astype(jnp.bfloat16)
    return upper, lower


def pool_matrix(window, width):
    shape = (width // window, window * width)
    out = lax.broadcasted_iota(jnp.int32, shape, 0)
    pixel = lax.broadcasted_iota(jnp.int32, shape, 1)
    inside = lax.div(lax.rem(pixel, width), window) == out
    return jnp.where(inside, 1.0 / (window * window), 0.0).astype(jnp.bfloat16)


def gather_kernel(count, scale, src_hbm, tgt_hbm, weight_hbm, bias_hbm,
                  all_ref, fine_ref, upper_ref, lower_ref, shift_ref, weight_ref, bias_ref,
                  tgt_ref, load_sem, send_sem, recv_sem):
    rows, width, hidden = tgt_ref.shape
    lines = count // 4
    me = lax.axis_index("tgt")
    core = lax.rem(me, 2)
    mate = me + 1 - 2 * core
    side = lax.rem(lax.div(me, 2), 2)
    beside = me + 2 - 4 * side
    line = lax.div(me, 4)
    place = me - 4 * line

    def along(step):
        return 4 * lax.rem(line + step, lines) + place

    barrier = pltpu.get_barrier_semaphore()
    peers = [along(step) for step in range(1, lines)] + [beside, mate]
    for peer in peers:
        pl.semaphore_signal(barrier, inc=1, device_id={"tgt": peer}, device_id_type=MESH)
    loads = [
        pltpu.make_async_copy(tgt_hbm, tgt_ref, load_sem.at[0]),
        pltpu.make_async_copy(weight_hbm, weight_ref, load_sem.at[1]),
        pltpu.make_async_copy(bias_hbm, bias_ref, load_sem.at[2]),
        pltpu.make_async_copy(src_hbm, all_ref.at[me, 0], load_sem.at[3]),
    ]
    for load in loads:
        load.start()
    pl.semaphore_wait(barrier, len(peers))

    sent = []
    slots = [0, 0]

    def copy(part, block, peer, slot, first=False):
        return pltpu.make_async_remote_copy(
            src_ref=src_hbm if first else all_ref.at[block, part],
            dst_ref=all_ref.at[block, part],
            send_sem=send_sem.at[part, slot],
            recv_sem=recv_sem.at[part, block],
            device_id={"tgt": peer},
            device_id_type=MESH,
        )

    def send(part, block, peer, first=False):
        one = copy(part, block, peer, slots[part], first)
        slots[part] += 1
        one.start()
        sent.append(one)

    def arrive(part, block):
        copy(part, block, mate, 0).wait_recv()

    def own(part):
        first = part == 0
        send(part, me, beside, first)
        for step in range(1, lines):
            send(part, me, along(step), first)
        send(part, me, mate, first)

    own(0)
    coarse = pool_matrix(4, width)
    loads[0].wait()
    pooled = []
    for row in range(0, rows, 4):
        pooled.append(dot(coarse, tgt_ref[row:row + 4].reshape(4 * width, hidden)))
    all_ref[me, 1] = jnp.concatenate(pooled, axis=0).astype(jnp.bfloat16)
    own(1)
    for load in loads[1:]:
        load.wait()
    for part in (0, 1):
        for step in range(1, lines):
            block = along(lines - step)
            arrive(part, block)
            send(part, block, beside)
            send(part, block, mate)
        if part == 0:
            fine = pool_matrix(2, width)
            half = width // 2
            for row in range(0, rows, 2):
                upper, lower = split_parts(dot(fine, tgt_ref[row:row + 2].reshape(2 * width, hidden)))
                feat = dot(upper, weight_ref[...]) + dot(lower, weight_ref[...]) + bias_ref[...]
                fine_ref[row // 2 * half:(row // 2 + 1) * half] = (feat * scale).astype(jnp.bfloat16)
    for part in (0, 1):
        for step in range(lines):
            block = along((lines - step) % lines) + 2 - 4 * side
            arrive(part, block)
            send(part, block, mate)
    feat = (dot(all_ref[me, 0], weight_ref[...]) + bias_ref[...]).astype(jnp.bfloat16)
    upper, lower = split_parts(dot_last(feat, weight_ref[...]) * scale)
    upper_ref[...] = upper
    lower_ref[...] = lower
    shift = jnp.sum(feat.astype(jnp.float32) * bias_ref[...], axis=1, keepdims=True) * scale
    shift_ref[...] = jnp.broadcast_to(shift, shift_ref.shape)
    for part in (0, 1):
        for step in range(lines):
            block = along((lines - step) % lines) + 1 - 2 * core
            arrive(part, block)
            arrive(part, block + 2 - 4 * side)
    for one in sent:
        one.wait_send()


def level_kernel(group, all_ref, fine_ref, upper_ref, lower_ref, shift_ref, weight_ref, bias_ref,
                 one_hbm, two_hbm, three_hbm, one_ref, two_ref, three_ref, sems):
    count, _, block, hidden = all_ref.shape
    copies = []
    wide = group * block
    narrow = wide // 4
    across = block // 2
    pixel = lax.broadcasted_iota(jnp.int32, (wide, narrow), 0)
    out = lax.broadcasted_iota(jnp.int32, (wide, narrow), 1)
    inside = (lax.div(pixel, block) * (across // 2) + lax.div(lax.rem(pixel, across), 2)) == out
    pool = jnp.where(inside, 0.25, 0.0).astype(jnp.bfloat16)

    def put(source, target):
        one = pltpu.make_async_copy(source, target, sems.at[len(copies)])
        one.start()
        copies.append(one)

    for step in range(count // group):
        stripes = slice(step * group, (step + 1) * group)
        at = slice(step * wide, (step + 1) * wide)
        src = all_ref[stripes, 0].reshape(wide, hidden)
        feat = (dot(src, weight_ref[...]) + bias_ref[...]).astype(jnp.bfloat16)
        one_ref[:, at] = dot_last(fine_ref[...], feat).astype(jnp.bfloat16)
        put(one_ref.at[:, at], one_hbm.at[:, at])
    for step in range(count // group):
        stripes = slice(step * group, (step + 1) * group)
        at = slice(step * wide, (step + 1) * wide)
        coarse = all_ref[stripes, 1].reshape(wide, hidden)
        two = dot_last(upper_ref[...], coarse) + dot_last(lower_ref[...], coarse)
        two = (two + shift_ref[:, :1]).astype(jnp.bfloat16)
        two_ref[:, at] = two
        three_ref[:, step * narrow:(step + 1) * narrow] = dot(two, pool).astype(jnp.bfloat16)
    put(two_ref, two_hbm)
    put(three_ref, three_hbm)
    for one in copies:
        one.wait()


def per_device(src_hidden, tgt_hidden, proj_weight, proj_bias):
    rows, width, hidden = tgt_hidden.shape
    channels = proj_weight.shape[1]
    count = lax.axis_size("tgt")
    own = src_hidden.shape[0]
    scale = 1.0 / math.sqrt(channels)
    fine_count = rows * width // 4
    group = 4
    bias = proj_bias.reshape(1, channels)
    vmem = pl.BlockSpec(memory_space=pltpu.VMEM)
    hbm = pl.BlockSpec(memory_space=pltpu.HBM)
    between = (
        jax.ShapeDtypeStruct((count, 2, own, hidden), jnp.bfloat16),
        jax.ShapeDtypeStruct((fine_count, channels), jnp.bfloat16),
        jax.ShapeDtypeStruct((own, hidden), jnp.bfloat16),
        jax.ShapeDtypeStruct((own, hidden), jnp.bfloat16),
        jax.ShapeDtypeStruct((own, 128), jnp.float32),
        jax.ShapeDtypeStruct(proj_weight.shape, jnp.bfloat16),
        jax.ShapeDtypeStruct(bias.shape, jnp.float32),
    )
    arguments = [
        pltpu.with_memory_space_constraint(one, pltpu.HBM)
        for one in (src_hidden, tgt_hidden, proj_weight, bias)
    ]
    gathered = pl.pallas_call(
        functools.partial(gather_kernel, count, scale),
        out_shape=between,
        in_specs=[hbm] * 4,
        out_specs=(vmem,) * len(between),
        scratch_shapes=[
            pltpu.VMEM(tgt_hidden.shape, jnp.bfloat16),
            pltpu.SemaphoreType.DMA((4,)),
            pltpu.SemaphoreType.DMA((2, count)),
            pltpu.SemaphoreType.DMA((2, count)),
        ],
        compiler_params=pltpu.CompilerParams(
            collective_id=0, has_side_effects=True, vmem_limit_bytes=32 * 1024 * 1024
        ),
        name="gather",
    )(*arguments)
    two_count = fine_count // 4 * count
    levels = (
        jax.ShapeDtypeStruct((fine_count, own * count), jnp.bfloat16),
        jax.ShapeDtypeStruct((own, two_count), jnp.bfloat16),
        jax.ShapeDtypeStruct((own, two_count // 4), jnp.bfloat16),
    )
    one, two, three = pl.pallas_call(
        functools.partial(level_kernel, group),
        out_shape=levels,
        in_specs=[vmem] * len(between),
        out_specs=(hbm,) * 3,
        scratch_shapes=[pltpu.VMEM(level.shape, level.dtype) for level in levels]
        + [pltpu.SemaphoreType.DMA((count // group + 2,))],
        compiler_params=pltpu.CompilerParams(vmem_limit_bytes=32 * 1024 * 1024),
        name="levels",
    )(*gathered)
    return one.reshape(rows // 2, width // 2, own * count), two, three


def solution(mesh):
    return jax.shard_map(
        per_device,
        mesh=mesh,
        in_specs=(P(("pairs", "tgt"), None), P(("pairs", "tgt"), None, None), P(), P()),
        out_specs=(
            P(("pairs", "tgt"), None, None),
            P(("pairs", "tgt"), None),
            P(("pairs", "tgt"), None),
        ),
        check_vma=False,
    )
```

time: 24.8 us -> 20.7 us (0.83)
  local copies, waits for them, and re-layouts: 3.31 us -> 0 us
  Pallas kernels: 20.5 us -> 19.9 us
    unnamed x8 -> x0, local copies, waits for them, and re-layouts: 3.31 us -> none
    pallas_call x1, Pallas kernels: 4.04 us -> 3.03 us  [per_device(): pl.pallas_call(functools.partial(level_kernel, group), out_shape=levels,...]
    pallas_call x1, Pallas kernels: 16.5 us -> 16.9 us  [per_device(): pl.pallas_call(functools.partial(gather_kernel, count, scale), out_shape=...]
where the time goes in v3:
time: 20.7 us; the launch traced here: 20.5 us
  Pallas kernels  19.9 us (96%)
  between operations  0.64 us (3%)
    pallas_call x1, Pallas kernels, per_device(): pl.pallas_call(functools.partial(gather_kernel, count, scale), out_shape=...  16.9 us
    pallas_call x1, Pallas kernels, per_device(): pl.pallas_call(functools.partial(level_kernel, group), out_shape=levels,...  3.03 us

profile of v3, /device:TPU:0, one launch (start us, length us, event | category | flops | bytes accessed | tf_op | source)
XLA Modules:
  0.0 20.5 jit_solution(11793261015774726785)
XLA Ops:
  0.6 16.9 %gather.1 = (bf16[16,2,128,128]{3,2,1,0:T(8,128)(2,1)S(1)}, bf16[512,256]{1,0:T(8,128)(2,1)S(1)}, bf16[128,128]{1,0:T(8,128)(2,1)S(1)}, bf16[128,128]{1,0:T(8,12...) custom-call(bf16[128,128]{1,0:T(8,128)(2,1)} %src_hbm.1, ...), custom_call_target="tpu_custom_call" | custom-call | tf_op jit(solution)/shard_map/gather/pallas_call | solution.py:201
  17.5 3.0 %levels.1 = (bf16[512,2048]{1,0:T(8,128)(2,1)}, bf16[128,2048]{1,0:T(8,128)(2,1)}, bf16[128,512]{1,0:T(8,128)(2,1)}) custom-call(bf16[16,2,128,128]{3,2,1,0:T(8,128)(2,1)S(1)} %get-tuple-element.13.all_ref, bf16[512,256]{1,0:T(8,128)(2,1)S(1)} %get-tuple-element.14.fine_ref, bf16[128,128]{1,0:T(8,128)(2,1)S(1)} %get-tuple-element.15.upper_ref, ...), custom_call_target="tpu_custom_call" | custom-call | tf_op jit(solution)/shard_map/levels/pallas_call | solution.py:223

commit v4 on v3

--- a/solution.py
+++ b/solution.py
@@ -38,20 +38,20 @@
                   all_ref, fine_ref, upper_ref, lower_ref, shift_ref, weight_ref, bias_ref,
                   tgt_ref, load_sem, send_sem, recv_sem):
     rows, width, hidden = tgt_ref.shape
-    lines = count // 4
+    lines = count // 8
     me = lax.axis_index("tgt")
-    core = lax.rem(me, 2)
-    mate = me + 1 - 2 * core
-    side = lax.rem(lax.div(me, 2), 2)
-    beside = me + 2 - 4 * side
-    line = lax.div(me, 4)
-    place = me - 4 * line
+    to_mate = 1 - 2 * lax.rem(me, 2)
+    to_beside = 2 - 4 * lax.rem(lax.div(me, 2), 2)
+    to_near = 4 - 8 * lax.rem(lax.div(me, 4), 2)
+    mate, beside, near = me + to_mate, me + to_beside, me + to_near
+    line = lax.div(me, 8)
+    place = me - 8 * line
 
     def along(step):
-        return 4 * lax.rem(line + step, lines) + place
+        return 8 * lax.rem(line + step, lines) + place
 
     barrier = pltpu.get_barrier_semaphore()
-    peers = [along(step) for step in range(1, lines)] + [beside, mate]
+    peers = [along(step) for step in range(1, lines)] + [near, beside, mate]
     for peer in peers:
         pl.semaphore_signal(barrier, inc=1, device_id={"tgt": peer}, device_id_type=MESH)
     loads = [
@@ -91,6 +91,7 @@
         send(part, me, beside, first)
         for step in range(1, lines):
             send(part, me, along(step), first)
+        send(part, me, near, first)
         send(part, me, mate, first)
 
     own(0)
@@ -103,24 +104,36 @@
     own(1)
     for load in loads[1:]:
         load.wait()
-    for part in (0, 1):
+    fine = pool_matrix(2, width)
+    half = width // 2
+    for part in (0, 1):
+        block = me + to_near
+        arrive(part, block)
+        send(part, block, beside)
+        send(part, block, mate)
         for step in range(1, lines):
             block = along(lines - step)
             arrive(part, block)
+            send(part, block, near)
             send(part, block, beside)
             send(part, block, mate)
         if part == 0:
-            fine = pool_matrix(2, width)
-            half = width // 2
             for row in range(0, rows, 2):
                 upper, lower = split_parts(dot(fine, tgt_ref[row:row + 2].reshape(2 * width, hidden)))
                 feat = dot(upper, weight_ref[...]) + dot(lower, weight_ref[...]) + bias_ref[...]
                 fine_ref[row // 2 * half:(row // 2 + 1) * half] = (feat * scale).astype(jnp.bfloat16)
     for part in (0, 1):
+        for step in range(1, lines):
+            block = along(lines - step) + to_near
+            arrive(part, block)
+            send(part, block, beside)
+            send(part, block, mate)
+    for part in (0, 1):
         for step in range(lines):
-            block = along((lines - step) % lines) + 2 - 4 * side
-            arrive(part, block)
-            send(part, block, mate)
+            block = along((lines - step) % lines) + to_beside
+            for block in (block, block + to_near):
+                arrive(part, block)
+                send(part, block, mate)
     feat = (dot(all_ref[me, 0], weight_ref[...]) + bias_ref[...]).astype(jnp.bfloat16)
     upper, lower = split_parts(dot_last(feat, weight_ref[...]) * scale)
     upper_ref[...] = upper
@@ -129,9 +142,10 @@
     shift_ref[...] = jnp.broadcast_to(shift, shift_ref.shape)
     for part in (0, 1):
         for step in range(lines):
-            block = along((lines - step) % lines) + 1 - 2 * core
-            arrive(part, block)
-            arrive(part, block + 2 - 4 * side)
+            block = along((lines - step) % lines) + to_mate
+            for block in (block, block + to_near):
+                arrive(part, block)
+                arrive(part, block + to_beside)
     for one in sent:
         one.wait_send()
 

time: 20.7 us -> 20.3 us (0.981)
  Pallas kernels: 19.9 us -> 19.5 us
    pallas_call x1, Pallas kernels: 16.9 us -> 16.5 us  [per_device(): pl.pallas_call(functools.partial(gather_kernel, count, scale), out_shape=...]
where the time goes in v4:
time: 20.3 us; the launch traced here: 20.2 us
  Pallas kernels  19.5 us (96%)
  between operations  0.64 us (3%)
    pallas_call x1, Pallas kernels, per_device(): pl.pallas_call(functools.partial(gather_kernel, count, scale), out_shape=...  16.5 us
    pallas_call x1, Pallas kernels, per_device(): pl.pallas_call(functools.partial(level_kernel, group), out_shape=levels,...  3.03 us

profile of v4, /device:TPU:0, one launch (start us, length us, event | category | flops | bytes accessed | tf_op | source)
XLA Modules:
  0.0 20.2 jit_solution(6231266361152886325)
XLA Ops:
  0.6 16.5 %gather.1 = (bf16[16,2,128,128]{3,2,1,0:T(8,128)(2,1)S(1)}, bf16[512,256]{1,0:T(8,128)(2,1)S(1)}, bf16[128,128]{1,0:T(8,128)(2,1)S(1)}, bf16[128,128]{1,0:T(8,12...) custom-call(bf16[128,128]{1,0:T(8,128)(2,1)} %src_hbm.1, ...), custom_call_target="tpu_custom_call" | custom-call | tf_op jit(solution)/shard_map/gather/pallas_call | solution.py:215
  17.2 3.0 %levels.1 = (bf16[512,2048]{1,0:T(8,128)(2,1)}, bf16[128,2048]{1,0:T(8,128)(2,1)}, bf16[128,512]{1,0:T(8,128)(2,1)}) custom-call(bf16[16,2,128,128]{3,2,1,0:T(8,128)(2,1)S(1)} %get-tuple-element.13.all_ref, bf16[512,256]{1,0:T(8,128)(2,1)S(1)} %get-tuple-element.14.fine_ref, bf16[128,128]{1,0:T(8,128)(2,1)S(1)} %get-tuple-element.15.upper_ref, ...), custom_call_target="tpu_custom_call" | custom-call | tf_op jit(solution)/shard_map/levels/pallas_call | solution.py:237

commit v5 on v4

--- a/solution.py
+++ b/solution.py
@@ -36,7 +36,7 @@
 
 def gather_kernel(count, scale, src_hbm, tgt_hbm, weight_hbm, bias_hbm,
                   all_ref, fine_ref, upper_ref, lower_ref, shift_ref, weight_ref, bias_ref,
-                  tgt_ref, load_sem, send_sem, recv_sem):
+                  one_ref, tgt_ref, load_sem, send_sem, recv_sem):
     rows, width, hidden = tgt_ref.shape
     lines = count // 8
     me = lax.axis_index("tgt")
@@ -93,6 +93,12 @@
             send(part, me, along(step), first)
         send(part, me, near, first)
         send(part, me, mate, first)
+
+    def level_one(block):
+        width = src_hbm.shape[0]
+        feat = (dot(all_ref[block, 0], weight_ref[...]) + bias_ref[...]).astype(jnp.bfloat16)
+        at = pl.ds(pl.multiple_of(block * width, width), width)
+        one_ref[:, at] = dot_last(fine_ref[...], feat).astype(jnp.bfloat16)
 
     own(0)
     coarse = pool_matrix(4, width)
@@ -122,12 +128,17 @@
                 upper, lower = split_parts(dot(fine, tgt_ref[row:row + 2].reshape(2 * width, hidden)))
                 feat = dot(upper, weight_ref[...]) + dot(lower, weight_ref[...]) + bias_ref[...]
                 fine_ref[row // 2 * half:(row // 2 + 1) * half] = (feat * scale).astype(jnp.bfloat16)
+    level_one(me)
+    level_one(near)
     for part in (0, 1):
         for step in range(1, lines):
             block = along(lines - step) + to_near
             arrive(part, block)
             send(part, block, beside)
             send(part, block, mate)
+    for step in range(1, lines):
+        level_one(along(step))
+        level_one(along(step) + to_near)
     for part in (0, 1):
         for step in range(lines):
             block = along((lines - step) % lines) + to_beside
@@ -140,40 +151,54 @@
     lower_ref[...] = lower
     shift = jnp.sum(feat.astype(jnp.float32) * bias_ref[...], axis=1, keepdims=True) * scale
     shift_ref[...] = jnp.broadcast_to(shift, shift_ref.shape)
-    for part in (0, 1):
-        for step in range(lines):
-            block = along((lines - step) % lines) + to_mate
-            for block in (block, block + to_near):
-                arrive(part, block)
-                arrive(part, block + to_beside)
+    for step in range(lines):
+        block = along((lines - step) % lines)
+        for block in (block, block + to_near):
+            level_one(block + to_beside)
+            arrive(0, block + to_mate)
+            level_one(block + to_mate)
+    for step in range(lines):
+        block = along((lines - step) % lines) + to_mate
+        for block in (block, block + to_near):
+            arrive(1, block)
+            arrive(0, block + to_beside)
+            arrive(1, block + to_beside)
     for one in sent:
         one.wait_send()
 
 
 def level_kernel(group, all_ref, fine_ref, upper_ref, lower_ref, shift_ref, weight_ref, bias_ref,
-                 one_hbm, two_hbm, three_hbm, one_ref, two_ref, three_ref, sems):
+                 early_ref, one_hbm, two_hbm, three_hbm, one_ref, two_ref, three_ref, sems):
     count, _, block, hidden = all_ref.shape
     copies = []
     wide = group * block
     narrow = wide // 4
     across = block // 2
+
+    def put(source, target):
+        one = pltpu.make_async_copy(source, target, sems.at[len(copies)])
+        one.start()
+        copies.append(one)
+
+    late = 3 - lax.rem(lax.axis_index("tgt"), 4)
+
+    def columns(index):
+        return pl.ds(pl.multiple_of(index * block, block), block)
+
+    for line in range(count // 4):
+        for other in range(1, 4):
+            at = columns(4 * line + lax.rem(late + other, 4))
+            put(early_ref.at[:, at], one_hbm.at[:, at])
+    for line in range(0, count // 4, 2):
+        src = [all_ref[4 * each + late, 0] for each in (line, line + 1)]
+        feat = (dot(jnp.concatenate(src, axis=0), weight_ref[...]) + bias_ref[...]).astype(jnp.bfloat16)
+        one_ref[:, line * block:(line + 2) * block] = dot_last(fine_ref[...], feat).astype(jnp.bfloat16)
+        for each in (line, line + 1):
+            put(one_ref.at[:, pl.ds(each * block, block)], one_hbm.at[:, columns(4 * each + late)])
     pixel = lax.broadcasted_iota(jnp.int32, (wide, narrow), 0)
     out = lax.broadcasted_iota(jnp.int32, (wide, narrow), 1)
     inside = (lax.div(pixel, block) * (across // 2) + lax.div(lax.rem(pixel, across), 2)) == out
     pool = jnp.where(inside, 0.25, 0.0).astype(jnp.bfloat16)
-
-    def put(source, target):
-        one = pltpu.make_async_copy(source, target, sems.at[len(copies)])
-        one.start()
-        copies.append(one)
-
-    for step in range(count // group):
-        stripes = slice(step * group, (step + 1) * group)
-        at = slice(step * wide, (step + 1) * wide)
-        src = all_ref[stripes, 0].reshape(wide, hidden)
-        feat = (dot(src, weight_ref[...]) + bias_ref[...]).astype(jnp.bfloat16)
-        one_ref[:, at] = dot_last(fine_ref[...], feat).astype(jnp.bfloat16)
-        put(one_ref.at[:, at], one_hbm.at[:, at])
     for step in range(count // group):
         stripes = slice(step * group, (step + 1) * group)
         at = slice(step * wide, (step + 1) * wide)
@@ -207,6 +232,7 @@
         jax.ShapeDtypeStruct((own, 128), jnp.float32),
         jax.ShapeDtypeStruct(proj_weight.shape, jnp.bfloat16),
         jax.ShapeDtypeStruct(bias.shape, jnp.float32),
+        jax.ShapeDtypeStruct((fine_count, own * count), jnp.bfloat16),
     )
     arguments = [
         pltpu.with_memory_space_constraint(one, pltpu.HBM)
@@ -239,8 +265,12 @@
         out_shape=levels,
         in_specs=[vmem] * len(between),
         out_specs=(hbm,) * 3,
-        scratch_shapes=[pltpu.VMEM(level.shape, level.dtype) for level in levels]
-        + [pltpu.SemaphoreType.DMA((count // group + 2,))],
+        scratch_shapes=[
+            pltpu.VMEM((fine_count, own * count // 4), jnp.bfloat16),
+            pltpu.VMEM((own, two_count), jnp.bfloat16),
+            pltpu.VMEM((own, two_count // 4), jnp.bfloat16),
+            pltpu.SemaphoreType.DMA((count + 2,)),
+        ],
         compiler_params=pltpu.CompilerParams(vmem_limit_bytes=32 * 1024 * 1024),
         name="levels",
     )(*gathered)

time: 20.3 us -> 21 us (1.034)
  Pallas kernels: 19.5 us -> 20.2 us
    pallas_call x1, Pallas kernels: 16.5 us -> 18 us  [per_device(): pl.pallas_call(functools.partial(gather_kernel, count, scale), out_shape=...]
    pallas_call x1, Pallas kernels: 3.03 us -> 2.16 us  [per_device(): pl.pallas_call(functools.partial(level_kernel, group), out_shape=levels,...]
where the time goes in v5:
time: 21 us; the launch traced here: 20.8 us
  Pallas kernels  20.2 us (96%)
  between operations  0.64 us (3%)
    pallas_call x1, Pallas kernels, per_device(): pl.pallas_call(functools.partial(gather_kernel, count, scale), out_shape=...  18 us
    pallas_call x1, Pallas kernels, per_device(): pl.pallas_call(functools.partial(level_kernel, group), out_shape=levels,...  2.16 us

profile of v5, /device:TPU:0, one launch (start us, length us, event | category | flops | bytes accessed | tf_op | source)
XLA Modules:
  0.0 20.8 jit_solution(10031609057979697600)
XLA Ops:
  0.6 18.0 %gather.1 = (bf16[16,2,128,128]{3,2,1,0:T(8,128)(2,1)S(1)}, bf16[512,256]{1,0:T(8,128)(2,1)S(1)}, bf16[128,128]{1,0:T(8,128)(2,1)S(1)}, bf16[128,128]{1,0:T(8,12...) custom-call(bf16[128,128]{1,0:T(8,128)(2,1)} %src_hbm.1, ...), custom_call_target="tpu_custom_call" | custom-call | tf_op jit(solution)/shard_map/gather/pallas_call | solution.py:241
  18.6 2.2 %levels.1 = (bf16[512,2048]{1,0:T(8,128)(2,1)}, bf16[128,2048]{1,0:T(8,128)(2,1)}, bf16[128,512]{1,0:T(8,128)(2,1)}) custom-call(bf16[16,2,128,128]{3,2,1,0:T(8,128)(2,1)S(1)} %get-tuple-element.14.all_ref, bf16[512,256]{1,0:T(8,128)(2,1)S(1)} %get-tuple-element.15.fine_ref, bf16[128,128]{1,0:T(8,128)(2,1)S(1)} %get-tuple-element.16.upper_ref, ...), custom_call_target="tpu_custom_call" | custom-call | tf_op jit(solution)/shard_map/levels/pallas_call | solution.py:263

commit v6 on v5

--- a/solution.py
+++ b/solution.py
@@ -128,17 +128,12 @@
                 upper, lower = split_parts(dot(fine, tgt_ref[row:row + 2].reshape(2 * width, hidden)))
                 feat = dot(upper, weight_ref[...]) + dot(lower, weight_ref[...]) + bias_ref[...]
                 fine_ref[row // 2 * half:(row // 2 + 1) * half] = (feat * scale).astype(jnp.bfloat16)
-    level_one(me)
-    level_one(near)
     for part in (0, 1):
         for step in range(1, lines):
             block = along(lines - step) + to_near
             arrive(part, block)
             send(part, block, beside)
             send(part, block, mate)
-    for step in range(1, lines):
-        level_one(along(step))
-        level_one(along(step) + to_near)
     for part in (0, 1):
         for step in range(lines):
             block = along((lines - step) % lines) + to_beside
@@ -154,15 +149,14 @@
     for step in range(lines):
         block = along((lines - step) % lines)
         for block in (block, block + to_near):
+            level_one(block)
             level_one(block + to_beside)
-            arrive(0, block + to_mate)
-            level_one(block + to_mate)
-    for step in range(lines):
-        block = along((lines - step) % lines) + to_mate
-        for block in (block, block + to_near):
-            arrive(1, block)
-            arrive(0, block + to_beside)
-            arrive(1, block + to_beside)
+    for part in (0, 1):
+        for step in range(lines):
+            block = along((lines - step) % lines) + to_mate
+            for block in (block, block + to_near):
+                arrive(part, block)
+                arrive(part, block + to_beside)
     for one in sent:
         one.wait_send()
 
@@ -180,21 +174,21 @@
         one.start()
         copies.append(one)
 
-    late = 3 - lax.rem(lax.axis_index("tgt"), 4)
+    core = lax.rem(lax.axis_index("tgt"), 2)
 
     def columns(index):
         return pl.ds(pl.multiple_of(index * block, block), block)
 
-    for line in range(count // 4):
-        for other in range(1, 4):
-            at = columns(4 * line + lax.rem(late + other, 4))
-            put(early_ref.at[:, at], one_hbm.at[:, at])
-    for line in range(0, count // 4, 2):
-        src = [all_ref[4 * each + late, 0] for each in (line, line + 1)]
-        feat = (dot(jnp.concatenate(src, axis=0), weight_ref[...]) + bias_ref[...]).astype(jnp.bfloat16)
-        one_ref[:, line * block:(line + 2) * block] = dot_last(fine_ref[...], feat).astype(jnp.bfloat16)
-        for each in (line, line + 1):
-            put(one_ref.at[:, pl.ds(each * block, block)], one_hbm.at[:, columns(4 * each + late)])
+    for pair in range(count // 2):
+        at = columns(2 * pair + core)
+        put(early_ref.at[:, at], one_hbm.at[:, at])
+    for first in range(0, count // 2, group):
+        pairs = range(first, first + group)
+        src = jnp.concatenate([all_ref[2 * pair + 1 - core, 0] for pair in pairs], axis=0)
+        feat = (dot(src, weight_ref[...]) + bias_ref[...]).astype(jnp.bfloat16)
+        one_ref[:, first * block:(first + group) * block] = dot_last(fine_ref[...], feat).astype(jnp.bfloat16)
+        for pair in pairs:
+            put(one_ref.at[:, pl.ds(pair * block, block)], one_hbm.at[:, columns(2 * pair + 1 - core)])
     pixel = lax.broadcasted_iota(jnp.int32, (wide, narrow), 0)
     out = lax.broadcasted_iota(jnp.int32, (wide, narrow), 1)
     inside = (lax.div(pixel, block) * (across // 2) + lax.div(lax.rem(pixel, across), 2)) == out
@@ -266,7 +260,7 @@
         in_specs=[vmem] * len(between),
         out_specs=(hbm,) * 3,
         scratch_shapes=[
-            pltpu.VMEM((fine_count, own * count // 4), jnp.bfloat16),
+            pltpu.VMEM((fine_count, own * count // 2), jnp.bfloat16),
             pltpu.VMEM((own, two_count), jnp.bfloat16),
             pltpu.VMEM((own, two_count // 4), jnp.bfloat16),
             pltpu.SemaphoreType.DMA((count + 2,)),

time: 21 us -> 20.4 us (0.971)
  Pallas kernels: 20.2 us -> 19.6 us
    pallas_call x1, Pallas kernels: 18 us -> 17.1 us  [per_device(): pl.pallas_call(functools.partial(gather_kernel, count, scale), out_shape=...]
    pallas_call x1, Pallas kernels: 2.16 us -> 2.49 us  [per_device(): pl.pallas_call(functools.partial(level_kernel, group), out_shape=levels,...]
where the time goes in v6:
time: 20.4 us; the launch traced here: 20.3 us
  Pallas kernels  19.6 us (96%)
  between operations  0.64 us (3%)
    pallas_call x1, Pallas kernels, per_device(): pl.pallas_call(functools.partial(gather_kernel, count, scale), out_shape=...  17.1 us
    pallas_call x1, Pallas kernels, per_device(): pl.pallas_call(functools.partial(level_kernel, group), out_shape=levels,...  2.49 us

profile of v6, /device:TPU:0, one launch (start us, length us, event | category | flops | bytes accessed | tf_op | source)
XLA Modules:
  0.0 20.3 jit_solution(7677867326152861157)
XLA Ops:
  0.6 17.1 %gather.1 = (bf16[16,2,128,128]{3,2,1,0:T(8,128)(2,1)S(1)}, bf16[512,256]{1,0:T(8,128)(2,1)S(1)}, bf16[128,128]{1,0:T(8,128)(2,1)S(1)}, bf16[128,128]{1,0:T(8,12...) custom-call(bf16[128,128]{1,0:T(8,128)(2,1)} %src_hbm.1, ...), custom_call_target="tpu_custom_call" | custom-call | tf_op jit(solution)/shard_map/gather/pallas_call | solution.py:235
  17.8 2.5 %levels.1 = (bf16[512,2048]{1,0:T(8,128)(2,1)}, bf16[128,2048]{1,0:T(8,128)(2,1)}, bf16[128,512]{1,0:T(8,128)(2,1)}) custom-call(bf16[16,2,128,128]{3,2,1,0:T(8,128)(2,1)S(1)} %get-tuple-element.14.all_ref, bf16[512,256]{1,0:T(8,128)(2,1)S(1)} %get-tuple-element.15.fine_ref, bf16[128,128]{1,0:T(8,128)(2,1)S(1)} %get-tuple-element.16.upper_ref, ...), custom_call_target="tpu_custom_call" | custom-call | tf_op jit(solution)/shard_map/levels/pallas_call | solution.py:257
